TPU v7x, 512 devices: a whole 4x4x16 slice. The times are simulated.
512 devices in a mesh: member: 16 (over y, z_hi), dp: 32 (over x, z_lo, core).
Axes of the slice: x: 4, y: 4, z: 16 (z_hi: 4, z_lo: 4; z = z_hi * 4 + z_lo), core: 2. Of those that a mesh axis runs over, the one named last changes fastest.
Arguments:
- features: bfloat16 [16, 512, 49, 1024], P('member', 'dp'), may hold values from -8 to 8
- labels: int32 [512], replicated, may hold values from 0 to 24575
- norm_gain: float32 [16, 1024], P('member'), may hold values from 0.75 to 1.25
- norm_bias: float32 [16, 1024], P('member'), may hold values from -0.25 to 0.25
- head_weight: bfloat16 [16, 1024, 24576], P('member', None, 'dp'), may hold values from -3 to 3
- head_bias: float32 [16, 24576], P('member', 'dp'), may hold values from -1.25 to 1.25
Outputs:
- mean_loss: float32 [], replicated
- grad_pooled: float32 [16, 512, 1024], P('member', 'dp')
- grad_gain: float32 [16, 1024], P('member')
- grad_bias: float32 [16, 1024], P('member')
- grad_head_weight: bfloat16 [16, 1024, 24576], P('member', None, 'dp')
- grad_head_bias: float32 [16, 24576], P('member', 'dp')
All inputs are finite; a program needn't handle non-finite values.
Results may differ from a plain program's by a relative error of at most 0.025.
Values may be sent and summed in bfloat16 or wider, within the bound.
No kernel may reach another device: no remote copies, remote signals or barrier semaphores. Data moves between devices by JAX's collectives and lax.ppermute only.
A program may use at most 64 MiB of HBM per device.

v0:
```python
import math
import jax
import jax.numpy as jnp
from jax import lax
from jax.sharding import PartitionSpec as P

norm_eps = 1e-06
loss_scale = 16.0


def merged(x, axis, combine):
    everything = jax.tree.map(lambda part: lax.all_gather(part, axis), x)
    initial = jax.tree.map(lambda part: part[0], everything)

    def hop(k, so_far):
        return combine(so_far, jax.tree.map(lambda part: part[k], everything))

    return lax.fori_loop(1, lax.axis_size(axis), hop, initial)


def layer_norm(pooled, norm_gain, norm_shift):
    center = pooled - jnp.mean(pooled, axis=-1, keepdims=True)
    inverse = lax.rsqrt(jnp.mean(center * center, axis=-1, keepdims=True) + norm_eps)
    normed = center * inverse
    return (normed, inverse, (normed * norm_gain + norm_shift).astype(jnp.bfloat16))


def norm_backward(upstream, normed, inverse, norm_gain):
    scaled = upstream * norm_gain
    return inverse * (
        scaled
        - jnp.mean(scaled, axis=-1, keepdims=True)
        - normed * jnp.mean(scaled * normed, axis=-1, keepdims=True)
    )


def member_join(former, latter):
    highest = jnp.maximum(former[0], latter[0])
    return (
        highest,
        former[1] * jnp.exp(former[0] - highest) + latter[1] * jnp.exp(latter[0] - highest),
    )


def per_device(features, labels, norm_gain, norm_bias, head_weight, head_bias):
    weight = head_weight[0]
    classes_here = weight.shape[1]
    gain_row = norm_gain[0]
    shift_row = norm_bias[0]
    position = lax.axis_index("dp")
    pooled = jnp.sum(features[0], axis=1, dtype=jnp.float32) / features.shape[2]
    normed, inverse, act = layer_norm(pooled, gain_row, shift_row)
    act_all = lax.all_gather(act, "dp", axis=0, tiled=True)
    logits = jnp.dot(act_all, weight, preferred_element_type=jnp.float32) + head_bias[0]
    local_class = labels - position * classes_here
    onehot = (local_class[:, None] == jnp.arange(classes_here, dtype=jnp.int32)[None, :]).astype(
        jnp.float32
    )
    label_part = jnp.sum(logits * onehot, axis=1)
    top_part = jnp.max(logits, axis=1)
    sum_part = jnp.sum(jnp.exp(logits - top_part[:, None]), axis=1)
    top_all = lax.pmax(top_part, "dp")
    sum_all, label_logit = lax.psum((sum_part * jnp.exp(top_part - top_all), label_part), "dp")
    log_total = top_all + jnp.log(sum_all)
    label_logp = label_logit - log_total
    mix_top, mix_sum = merged((label_logp, jnp.ones_like(label_logp)), "member", member_join)
    log_joint = mix_top + jnp.log(mix_sum)
    mean_loss = math.log(lax.axis_size("member")) - jnp.mean(log_joint)
    respons = jnp.exp(label_logp - log_joint)
    probabilities = jnp.exp(logits - log_total[:, None])
    grad_logits = (loss_scale * respons)[:, None] * (probabilities - onehot)
    grad_low = grad_logits.astype(jnp.bfloat16)
    grad_head_bias = jnp.sum(grad_logits, axis=0)
    grad_head_weight = lax.dot_general(
        act_all, grad_low, (((0,), (0,)), ((), ())), preferred_element_type=jnp.float32
    ).astype(jnp.bfloat16)
    upstream = lax.psum_scatter(
        lax.dot_general(
            grad_low, weight, (((1,), (1,)), ((), ())), preferred_element_type=jnp.float32
        ),
        "dp",
        scatter_dimension=0,
        tiled=True,
    )
    grad_gain, grad_shift = lax.psum(
        (jnp.sum(upstream * normed, axis=0), jnp.sum(upstream, axis=0)), "dp"
    )
    grad_pooled = norm_backward(upstream, normed, inverse, gain_row)
    return (
        mean_loss,
        grad_pooled[None],
        grad_gain[None],
        grad_shift[None],
        grad_head_weight[None],
        grad_head_bias[None],
    )


def solution(mesh):
    in_specs = (
        P("member", "dp", None, None),
        P(),
        P("member", None),
        P("member", None),
        P("member", None, "dp"),
        P("member", "dp"),
    )
    out_specs = (
        P(),
        P("member", "dp", None),
        P("member", None),
        P("member", None),
        P("member", None, "dp"),
        P("member", "dp"),
    )
    return jax.shard_map(
        per_device, mesh=mesh, in_specs=in_specs, out_specs=out_specs, check_vma=False
    )
```

profile of v0, /device:TPU:1, one launch (start us, length us, event | category | flops | bytes accessed | tf_op | source)
XLA Modules:
  0.0 497.9 jit_solution(16176686166835715571)
XLA Ops:
  7.2 0.0 copy-start
  7.2 0.0 copy-start.2
  7.2 0.0 copy-start.1
  7.2 0.0 copy-start.3
  7.2 0.0 copy-start.4
  7.2 0.0 all-gather.4.cloned.1.call-start
  7.3 1.8 convert_reduce_fusion
  9.0 0.1 multiply_reduce_fusion.4
  9.2 0.2 multiply_reduce_fusion.2
  9.4 0.0 copy-done.2
  9.4 0.0 copy-done.1
  9.4 0.7 add_convert_fusion
  10.1 0.0 all-gather.4.cloned.1.call-update
  10.1 0.0 reduce-scatter.2.cloned.1.call-start
  10.2 0.0 copy-done.3
  10.2 70.3 %all-gather.4.cloned.1.call-done = bf16[512,1024]{1,0:T(8,128)(2,1)} async-done(((bf16[16,1024]{1,0:T(8,128)(2,1)}), bf16[512,1024]{1,0:T(8,128)(2,1)}) %all-gather.4.cloned.1.call-update) | async-done | bytes 1048592 | tf_op jit(solution)/shard_map/all_gather | solution.py:53
  80.5 2.3 fusion.15
  82.8 67.0 %pmax.7 = f32[512]{0:T(512)S(1)} all-reduce(f32[512]{0:T(512)S(1)} %get-tuple-element.169), channel_id=1, replica_groups=mesh['member'=16,'dp'=32] {'dp'}, use_global_device_ids=true, to_apply=%region_6.0 | all-reduce | flops 512 | bytes 4096 | tf_op jit(solution)/shard_map/pmax | solution.py:62
  149.8 0.6 exponential_reduce_fusion
  150.4 70.2 %all-reduce.1 = (f32[512]{0:T(512)S(1)}, f32[512]{0:T(512)S(1)}) all-reduce(f32[512]{0:T(512)S(1)} %get-tuple-element.146, f32[512]{0:T(512)S(1)} %exponential_multiply_fusion.1), channel_id=1, replica_groups=mesh['member'=16,'dp'=32] {'dp'}, use_global_device_ids=true, to_apply=%region_4.0 | all-reduce | flops 1024 | bytes 8192 | tf_op jit(solution)/shard_map/psum | solution.py:63
  220.6 45.5 %all-gather.1 = f32[16,1,512]{2,1,0:T(1,128)S(1)} all-gather(f32[1,1,512]{2,1,0:T(1,128)S(1)} %bitcast.33), channel_id=2, replica_groups=mesh['member'=16,'dp'=32] {'member'}, dimensions={0}, use_global_device_ids=true | all-gather | bytes 34816 | tf_op jit(solution)/shard_map/all_gather | solution.py:12
  266.1 0.9 while.18
  267.0 0.6 exponential_multiply_fusion
  267.6 2.5 fusion.1
  270.1 0.0 reduce-scatter.2.cloned.1.call-update
  270.2 0.5 fusion.9
  270.7 0.6 broadcast_in_dim.28
  271.9 3.7 fusion.8
  275.6 138.1 %reduce-scatter.2.cloned.1.call-done = f32[16,1024]{1,0:T(8,128)} async-done(((f32[512,1024]{1,0:T(8,128)}), f32[16,1024]{1,0:T(8,128)}) %reduce-scatter.2.cloned.1.call-update) | async-done | bytes 65552 | tf_op jit(solution)/shard_map/reduce_scatter | solution.py:77
  413.7 1.0 multiply_reduce_fusion
  414.8 73.6 %all-reduce = (f32[1,1024]{1,0:T(1,128)}, f32[1,1024]{1,0:T(1,128)}) all-reduce(f32[1,1024]{1,0:T(1,128)S(1)} %bitcast.34, f32[1,1024]{1,0:T(1,128)S(1)} %bitcast.35), channel_id=1, replica_groups=mesh['member'=16,'dp'=32] {'dp'}, use_global_device_ids=true, to_apply=%region_16.0 | all-reduce | flops 2048 | bytes 16384 | tf_op jit(solution)/shard_map/psum | solution.py:85
  488.4 1.6 multiply_bitcast_fusion
  (42 shorter events, 0.5 us)
Async XLA Ops:
  7.2 73.4 %copy-start = (bf16[1,1024,768]{2,1,0:T(8,128)(2,1)S(1)}, bf16[1,1024,768]{2,1,0:T(8,128)(2,1)}, u32[]{:S(2)}) copy-start(bf16[1,1024,768]{2,1,0:T(8,128)(2,1)} %param.12) | copy-start | bytes 4718596
  7.2 2.2 copy-start.2
  7.2 2.2 copy-start.1
  7.2 3.0 copy-start.3
  7.2 3.0 copy-start.4
  7.2 73.3 %all-gather.4.cloned.1.call-start = ((), (), s32[]{:S(2)}) async-start(), calls=%async_computation.1 | async-start | bytes 1081344 | tf_op jit(solution)/shard_map/all_gather | solution.py:53
  10.1 403.6 %reduce-scatter.2.cloned.1.call-start = ((), (), s32[]{:S(2)}) async-start(), calls=%async_computation.2 | async-start | bytes 2162688 | tf_op jit(solution)/shard_map/reduce_scatter | solution.py:77
Sparse Core Ops, SparseCore 0:
  10.8 69.6 all-gather.3
  270.3 143.3 reduce-scatter.1
where the time goes:
time: 498 us
  blocking collectives  256 us (51%)
  waiting for transfers between devices  208 us (42%)
  between operations  16 us (3%)
  matrix products  8.5 us (2%)
  other arithmetic  7.42 us (1%)
    reduce_scatter x1, waiting for transfers between devices, per_device(): lax.psum_scatter(lax.dot_general(grad_low, weight, (((1,), (1,)), ((), ()...  138 us
    psum x1, blocking collectives, per_device(): lax.psum((jnp.sum(upstream * normed, axis=0), jnp.sum(upstream, axis=0)),...  73.6 us
    all_gather x1, waiting for transfers between devices, per_device(): act_all = lax.all_gather(act, 'dp', axis=0, tiled=True)  70.3 us
    psum x1, blocking collectives, per_device(): lax.psum((sum_part * jnp.exp(top_part - top_all), label_part), 'dp')  70.2 us
    pmax x1, blocking collectives, per_device(): top_all = lax.pmax(top_part, 'dp')  67 us
    all_gather x1, blocking collectives, merged(): everything = jax.tree.map(lambda part: lax.all_gather(part, axis), x)  45.5 us
  transfers between devices with their start and end apart: 2, of which 2 were waited for; matrix products, arithmetic and copies ran while one was open for 1% of the time, Pallas kernels for 0%

commit v1 on v0

--- a/solution.py
+++ b/solution.py
@@ -50,7 +50,9 @@
     position = lax.axis_index("dp")
     pooled = jnp.sum(features[0], axis=1, dtype=jnp.float32) / features.shape[2]
     normed, inverse, act = layer_norm(pooled, gain_row, shift_row)
-    act_all = lax.all_gather(act, "dp", axis=0, tiled=True)
+    act_all = jnp.concatenate(
+        lax.all_to_all(jnp.stack([act] * lax.axis_size("dp")), "dp", 0, 0), axis=0
+    )
     logits = jnp.dot(act_all, weight, preferred_element_type=jnp.float32) + head_bias[0]
     local_class = labels - position * classes_here
     onehot = (local_class[:, None] == jnp.arange(classes_here, dtype=jnp.int32)[None, :]).astype(

time: 498 us -> 470 us (0.944)
  waiting for transfers between devices: 208 us -> 166 us
  starting transfers between devices: 0.08 us -> 10.5 us
    all_gather x1 -> x0, waiting for transfers between devices: 70.3 us -> none  [per_device(): act_all = lax.all_gather(act, 'dp', axis=0, tiled=True)]
    all_to_all x0 -> x1, waiting for transfers between devices: none -> 27.9 us  [per_device(): lax.all_to_all(jnp.stack([act] * lax.axis_size('dp')), 'dp', 0, 0)]
    all_to_all x0 -> x1, starting transfers between devices: none -> 10.5 us  [per_device(): lax.all_to_all(jnp.stack([act] * lax.axis_size('dp')), 'dp', 0, 0)]
where the time goes in v1:
time: 470 us; the launch traced here: 469 us
  blocking collectives  258 us (55%)
  waiting for transfers between devices  166 us (35%)
  between operations  16 us (3%)
  starting transfers between devices  10.5 us (2%)
  matrix products  8.51 us (2%)
  other arithmetic  6.82 us (1%)
    reduce_scatter x1, waiting for transfers between devices, per_device(): lax.psum_scatter(lax.dot_general(grad_low, weight, (((1,), (1,)), ((), ()...  138 us
    psum x1, blocking collectives, per_device(): lax.psum((jnp.sum(upstream * normed, axis=0), jnp.sum(upstream, axis=0)),...  74 us
    psum x1, blocking collectives, per_device(): lax.psum((sum_part * jnp.exp(top_part - top_all), label_part), 'dp')  68.8 us
    pmax x1, blocking collectives, per_device(): top_all = lax.pmax(top_part, 'dp')  67 us
    all_gather x1, blocking collectives, merged(): everything = jax.tree.map(lambda part: lax.all_gather(part, axis), x)  48.2 us
    all_to_all x1, waiting for transfers between devices, per_device(): lax.all_to_all(jnp.stack([act] * lax.axis_size('dp')), 'dp', 0, 0)  27.9 us
    all_to_all x1, starting transfers between devices, per_device(): lax.all_to_all(jnp.stack([act] * lax.axis_size('dp')), 'dp', 0, 0)  10.5 us
  transfers between devices with their start and end apart: 2, of which 2 were waited for; matrix products, arithmetic and copies ran while one was open for 1% of the time, Pallas kernels for 0%

profile of v1, /device:TPU:1, one launch (start us, length us, event | category | flops | bytes accessed | tf_op | source)
XLA Modules:
  0.0 469.5 jit_solution(12146186090499567146)
XLA Ops:
  7.2 0.0 copy-start
  7.2 0.0 copy-start.3
  7.2 0.0 copy-start.2
  7.2 1.8 convert_reduce_fusion
  9.0 0.1 multiply_reduce_fusion.4
  9.1 0.2 multiply_reduce_fusion.2
  9.3 0.1 add_convert_fusion
  9.4 0.0 copy-start.4
  9.4 0.0 copy-start.5
  9.4 1.1 stack.2
  10.5 10.5 %all-to-all-start = ((bf16[32,16,1024]{2,1,0:T(8,128)(2,1)}), bf16[32,16,1024]{2,1,0:T(8,128)(2,1)S(1)}, u32[]{:S(2)}, u32[]{:S(2)}) async-start(bf16[32,16,1024]{2,1,0:T(8,128)(2,1)} %stack.2), calls=%async_computation | async-start | bytes 2097152 | tf_op jit(solution)/shard_map/all_to_all | solution.py:54
  21.0 0.0 reduce-scatter.2.cloned.1.call-start
  21.1 0.0 copy-done.5
  21.1 27.9 %all-to-all-done = bf16[32,16,1024]{2,1,0:T(8,128)(2,1)S(1)} async-done(((bf16[32,16,1024]{2,1,0:T(8,128)(2,1)}), bf16[32,16,1024]{2,1,0:T(8,128)(2,1)S(1)}, u32[]{:S(2)}, u32[]{:S(2)}) %all-to-all-start) | async-done | bytes 1048608 | tf_op jit(solution)/shard_map/all_to_all | solution.py:54
  49.0 1.0 copy-done.1
  50.0 0.0 copy-done
  50.0 2.3 fusion.15
  52.3 67.0 %pmax.7 = f32[512]{0:T(512)S(1)} all-reduce(f32[512]{0:T(512)S(1)} %get-tuple-element.169), channel_id=1, replica_groups=mesh['member'=16,'dp'=32] {'dp'}, use_global_device_ids=true, to_apply=%region_6.0 | all-reduce | flops 512 | bytes 4096 | tf_op jit(solution)/shard_map/pmax | solution.py:64
  119.3 0.6 exponential_reduce_fusion
  119.9 68.8 %all-reduce.1 = (f32[512]{0:T(512)S(1)}, f32[512]{0:T(512)S(1)}) all-reduce(f32[512]{0:T(512)S(1)} %get-tuple-element.146, f32[512]{0:T(512)S(1)} %exponential_multiply_fusion.1), channel_id=1, replica_groups=mesh['member'=16,'dp'=32] {'dp'}, use_global_device_ids=true, to_apply=%region_4.0 | all-reduce | flops 1024 | bytes 8192 | tf_op jit(solution)/shard_map/psum | solution.py:65
  188.7 48.2 %all-gather.1 = f32[16,1,512]{2,1,0:T(1,128)S(1)} all-gather(f32[1,1,512]{2,1,0:T(1,128)S(1)} %bitcast.36), channel_id=2, replica_groups=mesh['member'=16,'dp'=32] {'member'}, dimensions={0}, use_global_device_ids=true | all-gather | bytes 34816 | tf_op jit(solution)/shard_map/all_gather | solution.py:12
  236.9 0.9 while.18
  237.8 0.6 exponential_multiply_fusion
  238.5 2.6 fusion.1
  241.0 0.0 reduce-scatter.2.cloned.1.call-update
  241.0 0.5 fusion.9
  241.6 0.6 broadcast_in_dim.28
  242.8 3.7 fusion.8
  246.5 138.4 %reduce-scatter.2.cloned.1.call-done = f32[16,1024]{1,0:T(8,128)} async-done(((f32[512,1024]{1,0:T(8,128)}), f32[16,1024]{1,0:T(8,128)}) %reduce-scatter.2.cloned.1.call-update) | async-done | bytes 65552 | tf_op jit(solution)/shard_map/reduce_scatter | solution.py:79
  384.9 1.0 multiply_reduce_fusion
  386.0 74.0 %all-reduce = (f32[1,1024]{1,0:T(1,128)}, f32[1,1024]{1,0:T(1,128)}) all-reduce(f32[1,1024]{1,0:T(1,128)S(1)} %bitcast.37, f32[1,1024]{1,0:T(1,128)S(1)} %bitcast.38), channel_id=1, replica_groups=mesh['member'=16,'dp'=32] {'dp'}, use_global_device_ids=true, to_apply=%region_16.0 | all-reduce | flops 2048 | bytes 16384 | tf_op jit(solution)/shard_map/psum | solution.py:87
  460.0 1.6 multiply_bitcast_fusion
  (44 shorter events, 0.5 us)
Async XLA Ops:
  7.2 42.8 %copy-start = (bf16[1,1024,768]{2,1,0:T(8,128)(2,1)S(1)}, bf16[1,1024,768]{2,1,0:T(8,128)(2,1)}, u32[]{:S(2)}) copy-start(bf16[1,1024,768]{2,1,0:T(8,128)(2,1)} %param.12) | copy-start | bytes 4718596
  7.2 2.1 copy-start.3
  7.2 2.1 copy-start.2
  9.4 11.7 %copy-start.4 = (f32[1,768]{1,0:T(1,128)S(1)}, f32[1,768]{1,0:T(1,128)}, u32[]{:S(2)}) copy-start(f32[1,768]{1,0:T(1,128)} %param.13) | copy-start | bytes 9220
  9.4 11.7 %copy-start.5 = (s32[512]{0:T(512)S(1)}, s32[512]{0:T(512)}, u32[]{:S(2)}) copy-start(s32[512]{0:T(512)} %param.9) | copy-start | bytes 6148
  10.5 38.5 %all-to-all-start = ((bf16[32,16,1024]{2,1,0:T(8,128)(2,1)}), bf16[32,16,1024]{2,1,0:T(8,128)(2,1)S(1)}, u32[]{:S(2)}, u32[]{:S(2)}) async-start(bf16[32,16,1024]{2,1,0:T(8,128)(2,1)} %stack.2), calls=%async_computation | async-start | bytes 2097152 | tf_op jit(solution)/shard_map/all_to_all | solution.py:54
  21.0 363.9 %reduce-scatter.2.cloned.1.call-start = ((), (), s32[]{:S(2)}) async-start(), calls=%async_computation.2 | async-start | bytes 2162688 | tf_op jit(solution)/shard_map/reduce_scatter | solution.py:79
  49.0 1.0 copy-start.1
Sparse Core Ops, SparseCore 0:
  241.2 143.6 reduce-scatter.1
